TPU v7x, 32 devices: a whole 2x2x4 slice. The times are simulated.
32 devices in a mesh: groups: 2 (over y), ctx: 8 (over z, x), mp: 2 (over core).
Axes of the slice: x: 2, y: 2, z: 4, core: 2. Of those that a mesh axis runs over, the one named last changes fastest.
Arguments:
- queries: bfloat16 [4096, 2048], P(('groups', 'ctx'), 'mp'), parts along dimension 0, may hold values from -9 to 9
- keys_values: bfloat16 [2, 4096, 1024], P(None, ('groups', 'ctx'), 'mp'), parts along dimension 1, may hold values from -9 to 9
- out_grad: bfloat16 [4096, 2048], P(('groups', 'ctx'), 'mp'), parts along dimension 0, may hold values from -6 to 6
- doc_ids: int32 [4096], P(('groups', 'ctx')), parts along dimension 0, may hold values from 0 to 4, as said below
Outputs:
- attended: bfloat16 [4096, 2048], P(('groups', 'ctx'), 'mp'), parts along dimension 0
- query_grad: bfloat16 [4096, 2048], P(('groups', 'ctx'), 'mp'), parts along dimension 0
- pair_grad: bfloat16 [2, 4096, 1024], P(None, ('groups', 'ctx'), 'mp'), parts along dimension 1
There are 2 independent parts, one for each index of `groups`. A program takes and returns all parts, laid end to end along the dimension named above; each array names one. Nothing has to cross between parts.
Inputs may be any that keep to these rules, and one draw needn't show every extreme that they name: `doc_ids`: the sequence is a run of whole documents; all tokens of one document share a label, and the label rises by one from each document to the next, modulo 5, starting at 0. Every document holds at least 128 tokens (the first and the last may be shorter) and at most 512, and at least one holds exactly that many.
All inputs are finite; a program needn't handle non-finite values.
Results may differ from a plain program's by a relative error of at most 0.01.
Values may be sent and summed in bfloat16 or wider, within the bound.
A program may use at most 64 MiB of HBM per device.

v0:
```python
import jax
import jax.numpy as jnp
from jax import lax
from jax.sharding import PartitionSpec as P

HD = 128
DEPTH = 2


SCORE_SCALE = 144.0 ** (-0.5)
SOFT_CAP = 50.0


def from_behind(value, axis, steps):
    count = lax.axis_size(axis)
    first, last = (max(0, -steps), min(count, count - steps))
    return lax.ppermute(value, axis, [(source, source + steps) for source in range(first, last)])


def tile_logits(query_split, key_block):
    logits = (
        jnp.einsum("qhgd,khd->hgqk", query_split, key_block, preferred_element_type=jnp.float32)
        * SCORE_SCALE
    )
    return SOFT_CAP * jnp.tanh(logits / SOFT_CAP)


def guarded(runner, state):
    result = runner(state)
    return result


def per_device(queries, keys_values, out_grad, doc_ids):
    tok_rows = queries.shape[0]
    key_heads = keys_values.shape[2] // HD
    group_size = queries.shape[1] // HD // key_heads
    dev_index = lax.axis_index("ctx")
    query_split = queries.reshape(tok_rows, key_heads, group_size, HD)
    grad_split = out_grad.reshape(tok_rows, key_heads, group_size, HD)
    query_pos = dev_index * tok_rows + jnp.arange(tok_rows, dtype=jnp.int32)
    query_doc = doc_ids.astype(jnp.float32)
    home_block = (keys_values, doc_ids.astype(jnp.bfloat16))
    blocks = [home_block]
    current = home_block
    for offset in range(DEPTH):
        current = from_behind((current[0], current[1]), "ctx", 1)
        blocks.append(current)
    masks = []
    for distance in range(DEPTH + 1):
        key_pos = (dev_index - distance) * tok_rows + jnp.arange(tok_rows, dtype=jnp.int32)
        key_doc = blocks[distance][1].astype(jnp.float32)
        masks.append(
            (key_pos[None, :] <= query_pos[:, None])
            & (key_pos[None, :] >= 0)
            & (key_doc[None, :] == query_doc[:, None])
        )

    def split_pair(pair_block):
        return (
            pair_block[0].reshape(tok_rows, key_heads, HD),
            pair_block[1].reshape(tok_rows, key_heads, HD),
        )

    numerator = jnp.zeros((tok_rows, key_heads, group_size, HD), jnp.float32)
    denominator = jnp.zeros((key_heads, group_size, tok_rows), jnp.float32)
    for distance in range(DEPTH + 1):
        key_block, value_block = split_pair(blocks[distance][0])
        allowed = masks[distance]

        def forward_run(state, key_block=key_block, value_block=value_block, allowed=allowed):
            capped = tile_logits(query_split, key_block)
            exp_scores = jnp.where(allowed[None, None], jnp.exp(capped), 0.0)
            added = jnp.einsum(
                "hgqk,khd->qhgd",
                exp_scores.astype(jnp.bfloat16),
                value_block,
                preferred_element_type=jnp.float32,
            )
            return (state[0] + added, state[1] + jnp.sum(exp_scores, axis=3))

        numerator, denominator = guarded(forward_run, (numerator, denominator))
    attended = (numerator / jnp.transpose(denominator, (2, 0, 1))[..., None]).astype(jnp.bfloat16)
    grad_dot = jnp.sum(grad_split.astype(jnp.float32) * attended.astype(jnp.float32), axis=3)
    grad_dot_heads = jnp.transpose(grad_dot, (1, 2, 0))
    query_sum = jnp.zeros((tok_rows, key_heads, group_size, HD), jnp.float32)
    contribs = []
    for distance in range(DEPTH + 1):
        key_block, value_block = split_pair(blocks[distance][0])
        allowed = masks[distance]

        def backward_run(state, key_block=key_block, value_block=value_block, allowed=allowed):
            capped = tile_logits(query_split, key_block)
            exp_scores = jnp.where(allowed[None, None], jnp.exp(capped), 0.0)
            probability = exp_scores / denominator[..., None]
            grad_prob = jnp.einsum(
                "qhgd,khd->hgqk", grad_split, value_block, preferred_element_type=jnp.float32
            )
            grad_logit = (
                probability
                * (grad_prob - grad_dot_heads[..., None])
                * (1.0 - (capped / SOFT_CAP) ** 2)
            ).astype(jnp.bfloat16)
            query_part = jnp.einsum(
                "hgqk,khd->qhgd", grad_logit, key_block, preferred_element_type=jnp.float32
            )
            key_grad = (
                jnp.einsum(
                    "hgqk,qhgd->khd", grad_logit, query_split, preferred_element_type=jnp.float32
                )
                * SCORE_SCALE
            )
            value_grad = jnp.einsum(
                "hgqk,qhgd->khd",
                probability.astype(jnp.bfloat16),
                grad_split,
                preferred_element_type=jnp.float32,
            )
            stacked = jnp.stack(
                [
                    key_grad.reshape(tok_rows, key_heads * HD),
                    value_grad.reshape(tok_rows, key_heads * HD),
                ]
            )
            return (state[0] + query_part, stacked)

        empty_terms = jnp.zeros((2, tok_rows, key_heads * HD), jnp.float32)
        query_sum, terms = guarded(backward_run, (query_sum, empty_terms))
        contribs.append(terms)
    carried = contribs[DEPTH]
    for offset in range(DEPTH - 1, -1, -1):
        carried = from_behind(carried, "ctx", -1) + contribs[offset]
    attended_out = attended.reshape(tok_rows, key_heads * group_size * HD)
    query_grad = (
        (query_sum * SCORE_SCALE)
        .astype(jnp.bfloat16)
        .reshape(tok_rows, key_heads * group_size * HD)
    )
    return (attended_out, query_grad, carried.astype(jnp.bfloat16))


def solution(mesh):
    return jax.shard_map(
        per_device,
        mesh=mesh,
        in_specs=(
            P(("groups", "ctx"), "mp"),
            P(None, ("groups", "ctx"), "mp"),
            P(("groups", "ctx"), "mp"),
            P(("groups", "ctx")),
        ),
        out_specs=(
            P(("groups", "ctx"), "mp"),
            P(("groups", "ctx"), "mp"),
            P(None, ("groups", "ctx"), "mp"),
        ),
        check_vma=False,
    )
```

profile of v0, /device:TPU:0, one launch (start us, length us, event | category | flops | bytes accessed | tf_op | source)
XLA Modules:
  0.0 106.3 jit_solution(15826720528969862715)
XLA Ops:
  1.5 4.8 %collective-permute-start = (bf16[256]{0:T(256)(128)(2,1)S(1)}, bf16[256]{0:T(256)(128)(2,1)S(1)}, u32[]{:S(2)}, u32[]{:S(2)}) collective-permute-start(bf16[256]{0:T(256)(128)(2,1)S(1)} %get-tuple-element.10), channel_id=1, source_target_pairs={{0,2},{2,4},{4,6},{6,8},{8,10},{10,12},{12,14},{1,3},{3,5},{5,7},{... | collective-permute-start | bytes 1544 | tf_op jit(solution)/shard_map/ppermute | solution.py:17
  6.3 1.2 %copy.46 = bf16[2,256,512]{1,2,0:T(8,128)(2,1)S(1)} copy(bf16[2,256,512]{2,1,0:T(8,128)(2,1)} %param.5) | data formatting | bytes 1048576 | tf_op args[1]
  7.6 4.3 %collective-permute-start.1 = (bf16[2,256,512]{1,2,0:T(8,128)(2,1)S(1)}, bf16[2,256,512]{1,2,0:T(8,128)(2,1)}, u32[]{:S(2)}, u32[]{:S(2)}) collective-permute-start(bf16[2,256,512]{1,2,0:T(8,128)(2,1)S(1)} %copy.46), channel_id=1, source_target_pairs={{0,2},{2,4},{4,6},{6,8},{8,10},{10,12},{12,14},{1,3},{3,5},{5,7},{... | collective-permute-start | bytes 1572872 | tf_op jit(solution)/shard_map/ppermute | solution.py:17
  11.8 2.6 %collective-permute-start.2 = (bf16[256]{0:T(256)(128)(2,1)S(1)}, bf16[256]{0:T(256)(128)(2,1)S(1)}, u32[]{:S(2)}, u32[]{:S(2)}) collective-permute-start(bf16[256]{0:T(256)(128)(2,1)S(1)} %collective-permute-done), channel_id=1, source_target_pairs={{0,2},{2,4},{4,6},{6,8},{8,10},{10,12},{12,14},{1,3},{3,5},{5,7},{... | collective-permute-start | bytes 1544 | tf_op jit(solution)/shard_map/ppermute | solution.py:17
  15.1 6.8 %collective-permute-done.2 = bf16[256]{0:T(256)(128)(2,1)S(1)} collective-permute-done((bf16[256]{0:T(256)(128)(2,1)S(1)}, bf16[256]{0:T(256)(128)(2,1)S(1)}, u32[]{:S(2)}, u32[]{:S(2)}) %collective-permute-start.2) | collective-permute-done | bytes 544 | tf_op jit(solution)/shard_map/ppermute | solution.py:17
  24.0 1.1 %fusion.48 = (bf16[1,256,512]{1,2,0:T(8,128)(2,1)S(1)}, bf16[1,256,512]{1,2,0:T(8,128)(2,1)S(1)}) fusion(bf16[2,256,512]{1,2,0:T(8,128)(2,1)} %collective-permute-done.1), kind=kLoop, calls=%fused_computation.84 | loop fusion | bytes 1048576 | tf_op jit(solution)/shard_map/slice | solution.py:60
  25.0 4.5 %collective-permute-start.3 = (bf16[2,256,512]{1,2,0:T(8,128)(2,1)}, bf16[2,256,512]{1,2,0:T(8,128)(2,1)S(1)}, u32[]{:S(2)}, u32[]{:S(2)}) collective-permute-start(bf16[2,256,512]{1,2,0:T(8,128)(2,1)} %collective-permute-done.1), channel_id=1, source_target_pairs={{0,2},{2,4},{4,6},{6,8},{8,10},{10,12},{12,14},{1,3},{3,5},{5,7},{... | collective-permute-start | bytes 1572872 | tf_op jit(solution)/shard_map/ppermute | solution.py:17
  31.2 8.6 %collective-permute-done.3 = bf16[2,256,512]{1,2,0:T(8,128)(2,1)S(1)} collective-permute-done((bf16[2,256,512]{1,2,0:T(8,128)(2,1)}, bf16[2,256,512]{1,2,0:T(8,128)(2,1)S(1)}, u32[]{:S(2)}, u32[]{:S(2)}) %collective-permute-start.3) | collective-permute-done | bytes 524320 | tf_op jit(solution)/shard_map/ppermute | solution.py:17
  40.7 1.6 %fusion.19 = f32[4,256,128,1]{1,2,3,0:T(8,128)} fusion(bf16[256,4,2,128]{0,3,2,1:T(8,128)(2,1)S(1)} %bitcast.225, f32[4,2,256]{2,1,0:T(2,128)S(1)} %bitcast.239, f32[4,256,256,2]{2,1,3,0:T(8,128)S(1)} %get-tuple-element.20, pred[256,256]{0,1:T(8,128)(4,1)S(1)} %get-tuple-element.15), kind=kOutput, calls=%fused_computation.41 | convolution fusion | flops 136839168 | bytes 3219456 | tf_op jit(solution)/shard_map/hgqk,qhgd->khd/dot_general | solution.py:112
  42.3 1.6 %multiply_reduce_fusion = (f32[256,4,2]{0,2,1:T(2,128)S(1)}, bf16[256,4,2,128]{0,3,2,1:T(8,128)(2,1)}) fusion(bf16[256,1024]{0,1:T(8,128)(2,1)S(1)} %copy.58, f32[256,4,2]{0,2,1:T(2,128)S(1)} %bitcast.240, f32[4,2,256,128]{2,3,1,0:T(8,128)S(1)} %convolution_add_fusion.3, bf16[256,4,128,1]{0,2,3,1:T(8,128)(2,1)S(1)} %bitcast.237, ...), kind=kOutput, calls=%fused_computation.43 | convolution fusion | flops 138147840 | bytes 4538368 | tf_op jit(solution)/shard_map/hgqk,khd->qhgd/dot_general | solution.py:73
  43.9 1.1 %fusion = bf16[4,2,256,256]{2,3,1,0:T(8,128)(2,1)S(1)} fusion(f32[4,256,256,2]{2,1,3,0:T(8,128)S(1)} %get-tuple-element.20, bf16[256,4,128,1]{0,2,3,1:T(8,128)(2,1)S(1)} %bitcast.238, bf16[256,4,2,128]{0,3,2,1:T(8,128)(2,1)S(1)} %bitcast.226, f32[4,2,256]{2,1,0:T(2,128)S(1)} %bitcast.249, f32[4,2,256]{2,1,0:T(2,128)S(1)} %bitcast.241, ...), kind=kOutput, calls=%fused_computation.1 | convolution fusion | flops 139460608 | bytes 4014080 | tf_op jit(solution)/shard_map/qhgd,khd->hgqk/dot_general | solution.py:95
  45.0 1.1 %fusion.2 = bf16[4,2,256,256]{2,3,1,0:T(8,128)(2,1)S(1)} fusion(f32[4,256,256,2]{2,1,3,0:T(8,128)S(1)} %get-tuple-element.24, bf16[256,4,128,1]{0,2,3,1:T(8,128)(2,1)S(1)} %bitcast.220, bf16[256,4,2,128]{0,3,2,1:T(8,128)(2,1)S(1)} %bitcast.227, f32[4,2,256]{2,1,0:T(2,128)S(1)} %bitcast.250, f32[4,2,256]{2,1,0:T(2,128)S(1)} %bitcast.242, ...), kind=kOutput, calls=%fused_computation.5 | convolution fusion | flops 139460608 | bytes 4014080 | tf_op jit(solution)/shard_map/qhgd,khd->hgqk/dot_general | solution.py:95
  46.1 1.6 %fusion.17 = f32[4,256,128,1]{1,2,3,0:T(8,128)} fusion(bf16[256,4,2,128]{0,3,2,1:T(8,128)(2,1)S(1)} %bitcast.228, f32[4,2,256]{2,1,0:T(2,128)S(1)} %bitcast.243, f32[4,256,256,2]{2,1,3,0:T(8,128)S(1)} %get-tuple-element.24, pred[256,256]{0,1:T(8,128)(4,1)S(1)} %get-tuple-element.16), kind=kOutput, calls=%fused_computation.39 | convolution fusion | flops 136839168 | bytes 3219456 | tf_op jit(solution)/shard_map/hgqk,qhgd->khd/dot_general | solution.py:112
  49.0 1.1 %pad_maximum_fusion = f32[2,256,512]{2,1,0:T(8,128)} fusion(f32[1,256,512]{2,1,0:T(8,128)S(1)} %copy.72, f32[1,256,512]{2,1,0:T(8,128)S(1)} %copy.71), kind=kLoop, calls=%fused_computation.33 | loop fusion | flops 262144 | bytes 2097152 | tf_op jit(solution)/shard_map/stack | solution.py:118
  50.0 1.6 %collective-permute-start.4 = (f32[2,256,512]{2,1,0:T(8,128)}, f32[2,256,512]{2,1,0:T(8,128)}, u32[]{:S(2)}, u32[]{:S(2)}) collective-permute-start(f32[2,256,512]{2,1,0:T(8,128)} %pad_maximum_fusion), channel_id=1, source_target_pairs={{2,0},{4,2},{6,4},{8,6},{10,8},{12,10},{14,12},{3,1},{5,3},{7,5},{... | collective-permute-start | bytes 3145736 | tf_op jit(solution)/shard_map/ppermute | solution.py:17
  52.3 2.0 %copy.77 = f32[1,256,512]{2,1,0:T(8,128)} copy(f32[1,256,512]{1,2,0:T(8,128)} %bitcast.234) | data formatting | bytes 1048576 | tf_op jit(solution)/shard_map/stack;reshape | solution.py:118
  54.4 3.3 %fusion.15 = f32[4,256,128,1]{1,2,3,0:T(8,128)} fusion(bf16[256,4,2,128]{0,3,2,1:T(8,128)(2,1)S(1)} %bitcast.229, f32[4,2,256]{2,1,0:T(2,128)S(1)} %bitcast.244, f32[4,256,256,2]{2,1,3,0:T(8,128)} %copy-done.16, pred[256,256]{0,1:T(8,128)(4,1)S(1)} %get-tuple-element.17), kind=kOutput, calls=%fused_computation.37 | convolution fusion | flops 136839168 | bytes 3219456 | tf_op jit(solution)/shard_map/hgqk,qhgd->khd/dot_general | solution.py:112
  57.7 1.1 %fusion.4 = bf16[4,2,256,256]{2,3,1,0:T(8,128)(2,1)S(1)} fusion(f32[4,256,256,2]{2,1,3,0:T(8,128)S(1)} %copy-done.17, bf16[256,4,128,1]{0,2,3,1:T(8,128)(2,1)S(1)} %bitcast.236, bf16[256,4,2,128]{0,3,2,1:T(8,128)(2,1)S(1)} %bitcast.230, f32[4,2,256]{2,1,0:T(2,128)S(1)} %bitcast.251, f32[4,2,256]{2,1,0:T(2,128)S(1)} %bitcast.245, ...), kind=kOutput, calls=%fused_computation.9 | convolution fusion | flops 139460608 | bytes 4014080 | tf_op jit(solution)/shard_map/qhgd,khd->hgqk/dot_general | solution.py:95
  58.8 17.0 %collective-permute-done.4 = f32[2,256,512]{2,1,0:T(8,128)} collective-permute-done((f32[2,256,512]{2,1,0:T(8,128)}, f32[2,256,512]{2,1,0:T(8,128)}, u32[]{:S(2)}, u32[]{:S(2)}) %collective-permute-start.4) | collective-permute-done | bytes 1048608 | tf_op jit(solution)/shard_map/ppermute | solution.py:17
  75.8 2.4 %maximum_add_fusion = f32[2,256,512]{2,1,0:T(8,128)} fusion(f32[2,256,512]{2,1,0:T(8,128)} %collective-permute-done.4, f32[1,256,512]{2,1,0:T(8,128)S(1)} %copy-done.2, f32[1,256,512]{2,1,0:T(8,128)S(1)} %copy.76), kind=kLoop, calls=%fused_computation.34 | loop fusion | flops 524288 | bytes 3145728 | tf_op jit(solution)/shard_map/add | solution.py:131
  78.2 1.3 %collective-permute-start.5 = (f32[2,256,512]{2,1,0:T(8,128)}, f32[2,256,512]{2,1,0:T(8,128)}, u32[]{:S(2)}, u32[]{:S(2)}) collective-permute-start(f32[2,256,512]{2,1,0:T(8,128)} %maximum_add_fusion), channel_id=1, source_target_pairs={{2,0},{4,2},{6,4},{8,6},{10,8},{12,10},{14,12},{3,1},{5,3},{7,5},{... | collective-permute-start | bytes 3145736 | tf_op jit(solution)/shard_map/ppermute | solution.py:17
  80.2 1.2 %copy.82 = f32[1,256,512]{2,1,0:T(8,128)S(1)} copy(f32[1,256,512]{1,2,0:T(8,128)} %bitcast.232) | data formatting | bytes 1048576 | tf_op jit(solution)/shard_map/stack;reshape | solution.py:118
  86.0 18.1 %collective-permute-done.5 = f32[2,256,512]{2,1,0:T(8,128)} collective-permute-done((f32[2,256,512]{2,1,0:T(8,128)}, f32[2,256,512]{2,1,0:T(8,128)}, u32[]{:S(2)}, u32[]{:S(2)}) %collective-permute-start.5) | collective-permute-done | bytes 1048608 | tf_op jit(solution)/shard_map/ppermute | solution.py:17
  104.1 2.2 %fusion.14 = bf16[2,256,512]{2,1,0:T(8,128)(2,1)} fusion(f32[2,256,512]{2,1,0:T(8,128)} %collective-permute-done.5, f32[1,256,512]{2,1,0:T(8,128)S(1)} %copy.82, f32[1,256,512]{2,1,0:T(8,128)S(1)} %copy.81), kind=kLoop, calls=%fused_computation.36 | loop fusion | flops 786432 | bytes 2621440 | tf_op jit(solution)/shard_map/convert_element_type | solution.py:138
  (71 shorter events, 13.0 us)
Async XLA Ops:
  0.6 14.1 %slice-start = ((bf16[2,256,512]{2,1,0:T(8,128)(2,1)}), bf16[1,256,512]{2,1,0:T(8,128)(2,1)S(1)}, s32[]{:S(2)}) async-start(bf16[2,256,512]{2,1,0:T(8,128)(2,1)} %param.5), calls=%async_computation | async-start | bytes 524288 | tf_op jit(solution)/shard_map/slice | solution.py:61
  0.6 13.9 %copy-start.7 = (bf16[256,1024]{1,0:T(8,128)(2,1)S(1)}, bf16[256,1024]{1,0:T(8,128)(2,1)}, u32[]{:S(2)}) copy-start(bf16[256,1024]{1,0:T(8,128)(2,1)} %param.4) | copy-start | bytes 1572868
  0.7 14.2 %copy-start.8 = (bf16[256,1024]{1,0:T(8,128)(2,1)S(1)}, bf16[256,1024]{1,0:T(8,128)(2,1)}, u32[]{:S(2)}) copy-start(bf16[256,1024]{1,0:T(8,128)(2,1)} %param.6) | copy-start | bytes 1572868
  1.5 10.4 %collective-permute-start = (bf16[256]{0:T(256)(128)(2,1)S(1)}, bf16[256]{0:T(256)(128)(2,1)S(1)}, u32[]{:S(2)}, u32[]{:S(2)}) collective-permute-start(bf16[256]{0:T(256)(128)(2,1)S(1)} %get-tuple-element.10), channel_id=1, source_target_pairs={{0,2},{2,4},{4,6},{6,8},{8,10},{10,12},{12,14},{1,3},{3,5},{5,7},{... | collective-permute-start | bytes 1544 | tf_op jit(solution)/shard_map/ppermute | solution.py:17
  7.6 16.4 %collective-permute-start.1 = (bf16[2,256,512]{1,2,0:T(8,128)(2,1)S(1)}, bf16[2,256,512]{1,2,0:T(8,128)(2,1)}, u32[]{:S(2)}, u32[]{:S(2)}) collective-permute-start(bf16[2,256,512]{1,2,0:T(8,128)(2,1)S(1)} %copy.46), channel_id=1, source_target_pairs={{0,2},{2,4},{4,6},{6,8},{8,10},{10,12},{12,14},{1,3},{3,5},{5,7},{... | collective-permute-start | bytes 1572872 | tf_op jit(solution)/shard_map/ppermute | solution.py:17
  11.8 10.1 %collective-permute-start.2 = (bf16[256]{0:T(256)(128)(2,1)S(1)}, bf16[256]{0:T(256)(128)(2,1)S(1)}, u32[]{:S(2)}, u32[]{:S(2)}) collective-permute-start(bf16[256]{0:T(256)(128)(2,1)S(1)} %collective-permute-done), channel_id=1, source_target_pairs={{0,2},{2,4},{4,6},{6,8},{8,10},{10,12},{12,14},{1,3},{3,5},{5,7},{... | collective-permute-start | bytes 1544 | tf_op jit(solution)/shard_map/ppermute | solution.py:17
  14.9 8.3 %copy-start.14 = (bf16[1,256,512]{1,2,0:T(8,128)(2,1)}, bf16[1,256,512]{1,2,0:T(8,128)(2,1)S(1)}, u32[]{:S(2)}) copy-start(bf16[1,256,512]{1,2,0:T(8,128)(2,1)S(1)} %copy.49) | copy-start | bytes 786436
  15.1 31.0 %copy-start.9 = (bf16[256,1024]{0,1:T(8,128)(2,1)}, bf16[256,1024]{0,1:T(8,128)(2,1)S(1)}, u32[]{:S(2)}) copy-start(bf16[256,1024]{0,1:T(8,128)(2,1)S(1)} %copy.58) | copy-start | bytes 1572868
  23.2 1.9 %copy-start.16 = (f32[4,256,256,2]{2,1,3,0:T(8,128)}, f32[4,256,256,2]{2,1,3,0:T(8,128)S(1)}, u32[]{:S(2)}) copy-start(f32[4,256,256,2]{2,1,3,0:T(8,128)S(1)} %get-tuple-element.22) | copy-start | bytes 6291460
  25.0 6.1 %copy-start.3 = (bf16[1,256,512]{1,2,0:T(8,128)(2,1)}, bf16[1,256,512]{1,2,0:T(8,128)(2,1)S(1)}, u32[]{:S(2)}) copy-start(bf16[1,256,512]{1,2,0:T(8,128)(2,1)S(1)} %get-tuple-element.13) | copy-start | bytes 786436
  25.0 14.7 %collective-permute-start.3 = (bf16[2,256,512]{1,2,0:T(8,128)(2,1)}, bf16[2,256,512]{1,2,0:T(8,128)(2,1)S(1)}, u32[]{:S(2)}, u32[]{:S(2)}) collective-permute-start(bf16[2,256,512]{1,2,0:T(8,128)(2,1)} %collective-permute-done.1), channel_id=1, source_target_pairs={{0,2},{2,4},{4,6},{6,8},{8,10},{10,12},{12,14},{1,3},{3,5},{5,7},{... | collective-permute-start | bytes 1572872 | tf_op jit(solution)/shard_map/ppermute | solution.py:17
  39.8 2.4 %copy-start.5 = (bf16[1,256,512]{1,2,0:T(8,128)(2,1)}, bf16[1,256,512]{1,2,0:T(8,128)(2,1)S(1)}, u32[]{:S(2)}) copy-start(bf16[1,256,512]{1,2,0:T(8,128)(2,1)S(1)} %get-tuple-element.11) | copy-start | bytes 786436
  45.0 2.7 %copy-start = (bf16[4,2,256,256]{2,3,1,0:T(8,128)(2,1)}, bf16[4,2,256,256]{2,3,1,0:T(8,128)(2,1)S(1)}, u32[]{:S(2)}) copy-start(bf16[4,2,256,256]{2,3,1,0:T(8,128)(2,1)S(1)} %fusion) | copy-start | bytes 3145732
  47.7 1.0 copy-start.13
  50.0 4.3 %copy-start.10 = (bf16[256,1024]{0,1:T(8,128)(2,1)S(1)}, bf16[256,1024]{0,1:T(8,128)(2,1)}, u32[]{:S(2)}) copy-start(bf16[256,1024]{0,1:T(8,128)(2,1)} %copy-done.9) | copy-start | bytes 1572868
  50.0 25.8 %collective-permute-start.4 = (f32[2,256,512]{2,1,0:T(8,128)}, f32[2,256,512]{2,1,0:T(8,128)}, u32[]{:S(2)}, u32[]{:S(2)}) collective-permute-start(f32[2,256,512]{2,1,0:T(8,128)} %pad_maximum_fusion), channel_id=1, source_target_pairs={{2,0},{4,2},{6,4},{8,6},{10,8},{12,10},{14,12},{3,1},{5,3},{7,5},{... | collective-permute-start | bytes 3145736 | tf_op jit(solution)/shard_map/ppermute | solution.py:17
  54.4 3.3 %copy-start.11 = (bf16[256,1024]{0,1:T(8,128)(2,1)S(1)}, bf16[256,1024]{0,1:T(8,128)(2,1)}, u32[]{:S(2)}) copy-start(bf16[256,1024]{0,1:T(8,128)(2,1)} %copy-done.9) | copy-start | bytes 1572868
  54.4 3.3 %copy-start.15 = (bf16[1,256,512]{1,2,0:T(8,128)(2,1)S(1)}, bf16[1,256,512]{1,2,0:T(8,128)(2,1)}, u32[]{:S(2)}) copy-start(bf16[1,256,512]{1,2,0:T(8,128)(2,1)} %copy-done.14) | copy-start | bytes 786436
  54.4 3.3 %copy-start.17 = (f32[4,256,256,2]{2,1,3,0:T(8,128)S(1)}, f32[4,256,256,2]{2,1,3,0:T(8,128)}, u32[]{:S(2)}) copy-start(f32[4,256,256,2]{2,1,3,0:T(8,128)} %copy-done.16) | copy-start | bytes 6291460
  57.7 18.1 %copy-start.2 = (f32[1,256,512]{2,1,0:T(8,128)S(1)}, f32[1,256,512]{2,1,0:T(8,128)}, u32[]{:S(2)}) copy-start(f32[1,256,512]{2,1,0:T(8,128)} %copy.77) | copy-start | bytes 1572868
  78.2 25.9 %collective-permute-start.5 = (f32[2,256,512]{2,1,0:T(8,128)}, f32[2,256,512]{2,1,0:T(8,128)}, u32[]{:S(2)}, u32[]{:S(2)}) collective-permute-start(f32[2,256,512]{2,1,0:T(8,128)} %maximum_add_fusion), channel_id=1, source_target_pairs={{2,0},{4,2},{6,4},{8,6},{10,8},{12,10},{14,12},{3,1},{5,3},{7,5},{... | collective-permute-start | bytes 3145736 | tf_op jit(solution)/shard_map/ppermute | solution.py:17
  82.4 1.2 %copy-start.1 = (bf16[4,2,256,256]{2,3,1,0:T(8,128)(2,1)S(1)}, bf16[4,2,256,256]{2,3,1,0:T(8,128)(2,1)}, u32[]{:S(2)}) copy-start(bf16[4,2,256,256]{2,3,1,0:T(8,128)(2,1)} %copy-done) | copy-start | bytes 3145732
  82.4 1.3 %copy-start.6 = (bf16[1,256,512]{1,2,0:T(8,128)(2,1)S(1)}, bf16[1,256,512]{1,2,0:T(8,128)(2,1)}, u32[]{:S(2)}) copy-start(bf16[1,256,512]{1,2,0:T(8,128)(2,1)} %copy-done.5) | copy-start | bytes 786436
  83.7 1.3 %copy-start.12 = (bf16[256,4,2,128]{0,3,2,1:T(8,128)(2,1)S(1)}, bf16[256,4,2,128]{0,3,2,1:T(8,128)(2,1)}, u32[]{:S(2)}) copy-start(bf16[256,4,2,128]{0,3,2,1:T(8,128)(2,1)} %get-tuple-element.26) | copy-start | bytes 1572868
  (1 other events, 1.0 us)
where the time goes:
time: 107 us; the launch traced here: 106 us
  waiting for transfers between devices  50.5 us (47%)
  starting transfers between devices  19.1 us (18%)
  matrix products  17.8 us (17%)
  local copies, waits for them, and re-layouts  11 us (10%)
  other arithmetic  6.88 us (6%)
    ppermute x6, waiting for transfers between devices, from_behind(): lax.ppermute(value, axis, [(source, source + steps) for source in range(f...  50.5 us
    ppermute x6, starting transfers between devices, from_behind(): lax.ppermute(value, axis, [(source, source + steps) for source in range(f...  19.1 us
    dot_general x3, matrix products, backward_run(): jnp.einsum('hgqk,qhgd->khd', probability.astype(jnp.bfloat16), grad_split...  6.53 us
    unnamed x40, local copies, waits for them, and re-layouts  5.45 us
    another operation x6, local copies, waits for them, and re-layouts, backward_run(): jnp.stack([key_grad.reshape(tok_rows, key_heads * HD), value_grad.reshape...  4.06 us
    dot_general x3, matrix products, backward_run(): jnp.einsum('qhgd,khd->hgqk', grad_split, value_block, preferred_element_t...  3.24 us
    dot_general x3, matrix products, forward_run(): jnp.einsum('hgqk,khd->qhgd', exp_scores.astype(jnp.bfloat16), value_block...  3.18 us
    dot_general x3, matrix products, tile_logits(): jnp.einsum('qhgd,khd->hgqk', query_split, key_block, preferred_element_ty...  2.46 us
  transfers between devices with their start and end apart: 6, of which 4 were waited for; matrix products, arithmetic and copies ran while one was open for 16% of the time, Pallas kernels for 0%

commit v1 on v0

v1 whole, which is shorter than its diff:
```python
import functools
import math

import jax
import jax.numpy as jnp
from jax import lax
from jax.experimental import pallas as pl
from jax.experimental.pallas import tpu as pltpu
from jax.sharding import PartitionSpec as P

HD = 128
DEPTH = 2
SCORE_SCALE = 144.0 ** (-0.5)
SOFT_CAP = 50.0
TANH_SCALE = SCORE_SCALE / SOFT_CAP
EXP2_SCALE = SOFT_CAP * math.log2(math.e)

MESH = pl.DeviceIdType.MESH
F32 = jnp.float32
BF16 = jnp.bfloat16


def dot_nt(a, b):
    return lax.dot_general(a, b, (((1,), (1,)), ((), ())), preferred_element_type=F32)


def dot_nn(a, b):
    return lax.dot_general(a, b, (((1,), (0,)), ((), ())), preferred_element_type=F32)


def kernel(
    n, rows, heads, group,
    q_ref, kv_ref, do_ref, doc_ref,
    att_ref, dq_ref, dkv_ref,
    kv_in, doc_in, grad_out, grad_in, mask, exps, weights, own,
    kv_send, kv_recv, doc_send, doc_recv, grad_send, grad_recv,
):
    me = lax.axis_index("ctx")
    barrier = pltpu.get_barrier_semaphore()
    for d in range(1, DEPTH + 1):
        @pl.when(me >= d)
        def _(d=d):
            pl.semaphore_signal(barrier, inc=1, device_id={"ctx": me - d}, device_id_type=MESH)

        @pl.when(me + d < n)
        def _(d=d):
            pl.semaphore_signal(barrier, inc=1, device_id={"ctx": me + d}, device_id_type=MESH)

    peers = jnp.minimum(me, DEPTH) + jnp.minimum(n - 1 - me, DEPTH)
    pl.semaphore_wait(barrier, peers)

    def doc_copy(d):
        return pltpu.make_async_remote_copy(
            src_ref=doc_ref, dst_ref=doc_in.at[d - 1],
            send_sem=doc_send.at[d - 1], recv_sem=doc_recv.at[d - 1],
            device_id={"ctx": me + d}, device_id_type=MESH,
        )

    def head_cols(h):
        return pl.ds(pl.multiple_of(h * HD, HD), HD)

    def kv_copy(d, h):
        return pltpu.make_async_remote_copy(
            src_ref=kv_ref.at[:, :, head_cols(h)], dst_ref=kv_in.at[d - 1, h],
            send_sem=kv_send.at[d - 1, h], recv_sem=kv_recv.at[d - 1, h],
            device_id={"ctx": me + d}, device_id_type=MESH,
        )

    def grad_copy(d, h):
        return pltpu.make_async_remote_copy(
            src_ref=grad_out.at[d - 1, h], dst_ref=grad_in.at[d - 1, h],
            send_sem=grad_send.at[d - 1, h], recv_sem=grad_recv.at[d - 1, h],
            device_id={"ctx": me - d}, device_id_type=MESH,
        )

    for d in range(1, DEPTH + 1):
        @pl.when(me + d < n)
        def _(d=d):
            doc_copy(d).start()

    for h in range(heads):
        for d in range(1, DEPTH + 1):
            @pl.when(me + d < n)
            def _(d=d, h=h):
                kv_copy(d, h).start()

    for d in range(1, DEPTH + 1):
        @pl.when(me < d)
        def _(d=d):
            kv_in[d - 1] = jnp.zeros(kv_in.shape[1:], BF16)
            doc_in[d - 1] = jnp.full(doc_in.shape[1:], -1, jnp.int32)

        @pl.when(me + d >= n)
        def _(d=d):
            grad_in[d - 1] = jnp.zeros(grad_in.shape[1:], BF16)

    query_doc = jnp.broadcast_to(doc_ref[...].astype(F32), (rows, rows))

    def key_column(docs):
        column = jnp.transpose(jnp.broadcast_to(docs.astype(F32), (HD, rows)))
        return jnp.concatenate([column] * (rows // HD), axis=1)

    key_index = lax.broadcasted_iota(jnp.int32, (rows, rows), 0)
    query_index = lax.broadcasted_iota(jnp.int32, (rows, rows), 1)
    mask[0] = jnp.where(
        (key_column(doc_ref[...]) == query_doc) & (key_index <= query_index), 1.0, 0.0
    )
    for d in range(1, DEPTH + 1):
        @pl.when(me >= d)
        def _(d=d):
            doc_copy(d).wait_recv()

        mask[d] = jnp.where(key_column(doc_in[d - 1]) == query_doc, 1.0, 0.0)

    def head_step(h, carry):
        cols = head_cols(h)
        query_cols = [head_cols(h * group + g) for g in range(group)]
        queries = jnp.concatenate([q_ref[:, c] for c in query_cols], axis=0)
        grads = jnp.concatenate([do_ref[:, c] for c in query_cols], axis=0)
        width = group * rows
        numerator = jnp.zeros((HD, width), F32)
        sums = [jnp.zeros((1, rows), F32) for _ in range(group)]

        def block(d, which):
            if d == 0:
                return kv_ref[which, :, cols]
            return kv_in[d - 1, h, which]

        for d in range(DEPTH + 1):
            if d > 0:
                @pl.when(me >= d)
                def _(d=d):
                    kv_copy(d, h).wait_recv()

            scores = dot_nt(block(d, 0), queries)
            for g in range(group):
                span = slice(g * rows, (g + 1) * rows)
                capped = jnp.tanh(scores[:, span] * TANH_SCALE)
                exp_scores = jnp.exp2(capped * EXP2_SCALE) * mask[d]
                weights[d, :, span] = exp_scores - exp_scores * (capped * capped)
                sums[g] = sums[g] + jnp.sum(exp_scores, axis=0, keepdims=True)
                exps[d, :, span] = exp_scores.astype(BF16)
            numerator = numerator + dot_nn(jnp.transpose(block(d, 1)), exps[d])

        inverse = 1.0 / jnp.concatenate(sums, axis=1)
        attended = (numerator * inverse).astype(BF16)
        grad_dot = jnp.sum(
            jnp.transpose(grads).astype(F32) * attended.astype(F32), axis=0, keepdims=True
        )
        for g in range(group):
            att_ref[:, query_cols[g]] = jnp.transpose(attended[:, g * rows:(g + 1) * rows])
        inverse_column = jnp.transpose(jnp.broadcast_to(inverse, (HD, width)))
        grads_scaled = (grads.astype(F32) * inverse_column).astype(BF16)

        query_sum = jnp.zeros((HD, width), F32)
        for d in range(DEPTH, -1, -1):
            grad_prob = dot_nt(block(d, 1), grads)
            grad_logit = (weights[d] * ((grad_prob - grad_dot) * inverse)).astype(BF16)
            key_grad = dot_nn(grad_logit, queries) * SCORE_SCALE
            value_grad = dot_nn(exps[d], grads_scaled)
            if d == 0:
                own[h, 0] = key_grad
                own[h, 1] = value_grad
            else:
                grad_out[d - 1, h, 0] = key_grad.astype(BF16)
                grad_out[d - 1, h, 1] = value_grad.astype(BF16)

                @pl.when(me >= d)
                def _(d=d):
                    grad_copy(d, h).start()

            query_sum = query_sum + dot_nn(jnp.transpose(block(d, 0)), grad_logit)
        query_grad = (query_sum * SCORE_SCALE).astype(BF16)
        for g in range(group):
            dq_ref[:, query_cols[g]] = jnp.transpose(query_grad[:, g * rows:(g + 1) * rows])
        return carry

    lax.fori_loop(0, heads, head_step, 0)

    def finish(h, carry):
        for d in range(1, DEPTH + 1):
            @pl.when(me + d < n)
            def _(d=d):
                grad_copy(d, h).wait_recv()

        total = own[h]
        for d in range(1, DEPTH + 1):
            total = total + grad_in[d - 1, h].astype(F32)
        dkv_ref[:, :, head_cols(h)] = total.astype(BF16)
        return carry

    lax.fori_loop(0, heads, finish, 0)

    for d in range(1, DEPTH + 1):
        @pl.when(me + d < n)
        def _(d=d):
            doc_copy(d).wait_send()

    def drain(h, carry):
        for d in range(1, DEPTH + 1):
            @pl.when(me + d < n)
            def _(d=d):
                kv_copy(d, h).wait_send()

            @pl.when(me >= d)
            def _(d=d):
                grad_copy(d, h).wait_send()
        return carry

    lax.fori_loop(0, heads, drain, 0)


def per_device(queries, keys_values, out_grad, doc_ids):
    rows = queries.shape[0]
    heads = keys_values.shape[2] // HD
    group = queries.shape[1] // HD // heads
    n = lax.axis_size("ctx")
    slot = (DEPTH, heads, 2, rows, HD)
    vmem = pl.BlockSpec(memory_space=pltpu.VMEM)
    dma = pltpu.SemaphoreType.DMA
    return pl.pallas_call(
        functools.partial(kernel, n, rows, heads, group),
        out_shape=(
            jax.ShapeDtypeStruct(queries.shape, BF16),
            jax.ShapeDtypeStruct(queries.shape, BF16),
            jax.ShapeDtypeStruct(keys_values.shape, BF16),
        ),
        in_specs=[vmem] * 4,
        out_specs=(vmem,) * 3,
        scratch_shapes=[
            pltpu.VMEM(slot, BF16),
            pltpu.VMEM((DEPTH, 1, rows), jnp.int32),
            pltpu.VMEM(slot, BF16),
            pltpu.VMEM(slot, BF16),
            pltpu.VMEM((DEPTH + 1, rows, rows), F32),
            pltpu.VMEM((DEPTH + 1, rows, group * rows), BF16),
            pltpu.VMEM((DEPTH + 1, rows, group * rows), F32),
            pltpu.VMEM((heads, 2, rows, HD), F32),
            dma((DEPTH, heads)), dma((DEPTH, heads)),
            dma((DEPTH,)), dma((DEPTH,)),
            dma((DEPTH, heads)), dma((DEPTH, heads)),
        ],
        compiler_params=pltpu.CompilerParams(
            collective_id=0, has_side_effects=True, vmem_limit_bytes=40 * 1024 * 1024
        ),
        name="packed_attention",
    )(queries, keys_values, out_grad, doc_ids.reshape(1, rows))


def solution(mesh):
    return jax.shard_map(
        per_device,
        mesh=mesh,
        in_specs=(
            P(("groups", "ctx"), "mp"),
            P(None, ("groups", "ctx"), "mp"),
            P(("groups", "ctx"), "mp"),
            P(("groups", "ctx")),
        ),
        out_specs=(
            P(("groups", "ctx"), "mp"),
            P(("groups", "ctx"), "mp"),
            P(None, ("groups", "ctx"), "mp"),
        ),
        check_vma=False,
    )
```

time: 107 us -> 39.1 us (0.37)
  waiting for transfers between devices: 50.5 us -> 0 us
  Pallas kernels: 0 us -> 32 us
  starting transfers between devices: 19.1 us -> 0 us
  matrix products: 17.8 us -> 0 us
  other arithmetic: 6.88 us -> 0 us
  local copies, waits for them, and re-layouts: 11 us -> 6.18 us
    ppermute x6 -> x0, waiting for transfers between devices: 50.5 us -> none  [from_behind(): lax.ppermute(value, axis, [(source, source + steps) for source in range(f...]
    pallas_call x0 -> x1, Pallas kernels: none -> 32 us  [per_device(): pl.pallas_call(functools.partial(kernel, n, rows, heads, group), out_shap...]
    ppermute x6 -> x0, starting transfers between devices: 19.1 us -> none  [from_behind(): lax.ppermute(value, axis, [(source, source + steps) for source in range(f...]
    dot_general x18 -> x0, matrix products: 17.8 us -> none  [the longest x3 6.53 us: backward_run(): jnp.einsum('hgqk,qhgd->khd', probability.astype(jnp.bfloat16), grad_split...]
    another operation x6 -> x0, local copies, waits for them, and re-layouts: 4.06 us -> none  [backward_run(): jnp.stack([key_grad.reshape(tok_rows, key_heads * HD), value_grad.reshape...]
    convert_element_type x4 -> x0, other arithmetic: 2.97 us -> none  [the longest x1 2.17 us: per_device(): return (attended_out, query_grad, carried.astype(jnp.bfloat16))]
    add x4 -> x0, other arithmetic: 2.44 us -> none  [the longest x1 2.42 us: per_device(): carried = from_behind(carried, 'ctx', -1) + contribs[offset]]
    slice x6 -> x0, local copies, waits for them, and re-layouts: 1.26 us -> none  [the longest x3 1.12 us: split_pair(): pair_block[0].reshape(tok_rows, key_heads, HD)]
  transfers between devices with their start and end apart: 6 -> 0, of which waited for: 4 -> 0; matrix products, arithmetic and copies ran while one was open for 16% -> 0% of each run, Pallas kernels for 0% -> 0%
where the time goes in v1:
time: 39.1 us; the launch traced here: 38.8 us
  Pallas kernels  32 us (82%)
  local copies, waits for them, and re-layouts  6.18 us (16%)
  between operations  0.65 us (2%)
    pallas_call x1, Pallas kernels, per_device(): pl.pallas_call(functools.partial(kernel, n, rows, heads, group), out_shap...  32 us
    unnamed x11, local copies, waits for them, and re-layouts  6.18 us

profile of v1, /device:TPU:0, one launch (start us, length us, event | category | flops | bytes accessed | tf_op | source)
XLA Modules:
  0.0 38.8 jit_solution(8932440402461772791)
XLA Ops:
  0.6 0.0 copy-start.3
  0.6 0.7 %copy-done.3 = s32[256]{0:T(256)S(1)} copy-done((s32[256]{0:T(256)S(1)}, s32[256]{0:T(256)}, u32[]{:S(2)}) %copy-start.3) | copy-done | bytes 1048
  1.3 0.0 copy-start
  1.3 1.0 %copy-done = bf16[256,1024]{1,0:T(8,128)(2,1)S(1)} copy-done((bf16[256,1024]{1,0:T(8,128)(2,1)S(1)}, bf16[256,1024]{1,0:T(8,128)(2,1)}, u32[]{:S(2)}) %copy-start) | copy-done | bytes 524312
  2.4 0.0 copy-start.1
  2.4 1.0 %copy-done.1 = bf16[2,256,512]{2,1,0:T(8,128)(2,1)S(1)} copy-done((bf16[2,256,512]{2,1,0:T(8,128)(2,1)S(1)}, bf16[2,256,512]{2,1,0:T(8,128)(2,1)}, u32[]{:S(2)}) %copy-start.1) | copy-done | bytes 524312
  3.4 0.0 copy-start.2
  3.4 1.0 %copy-done.2 = bf16[256,1024]{1,0:T(8,128)(2,1)S(1)} copy-done((bf16[256,1024]{1,0:T(8,128)(2,1)S(1)}, bf16[256,1024]{1,0:T(8,128)(2,1)}, u32[]{:S(2)}) %copy-start.2) | copy-done | bytes 524312
  4.4 32.0 %packed_attention.1 = (bf16[256,1024]{1,0:T(8,128)(2,1)S(1)}, bf16[256,1024]{1,0:T(8,128)(2,1)S(1)}, bf16[2,256,512]{2,1,0:T(8,128)(2,1)S(1)}) custom-call(bf16[256,1024]{1,0:T(8,128)(2,1)S(1)} %copy-done, bf16[2,256,512]{2,1,0:T(8,128)(2,1)S(1)} %copy-done.1, bf16[256,1024]{1,0:T(8,128)(2,1)S(1)} %copy-done.2, s32[1,256]{1,0:T(1,128)S(1)} %bitcast.1), custom_call_target="tpu_custom_call" | custom-call | tf_op jit(solution)/shard_map/packed_attention/pallas_call | solution.py:221
  36.5 0.8 %copy.10 = bf16[256,1024]{1,0:T(8,128)(2,1)} copy(bf16[256,1024]{1,0:T(8,128)(2,1)S(1)} %get-tuple-element.6) | data formatting | bytes 1048576
  37.3 0.8 %copy.11 = bf16[256,1024]{1,0:T(8,128)(2,1)} copy(bf16[256,1024]{1,0:T(8,128)(2,1)S(1)} %get-tuple-element.7) | data formatting | bytes 1048576
  38.1 0.8 %copy.12 = bf16[2,256,512]{2,1,0:T(8,128)(2,1)} copy(bf16[2,256,512]{2,1,0:T(8,128)(2,1)S(1)} %get-tuple-element.8) | data formatting | bytes 1048576
Async XLA Ops:
  0.6 0.7 %copy-start.3 = (s32[256]{0:T(256)S(1)}, s32[256]{0:T(256)}, u32[]{:S(2)}) copy-start(s32[256]{0:T(256)} %param.7) | copy-start | bytes 3076
  1.3 1.0 %copy-start = (bf16[256,1024]{1,0:T(8,128)(2,1)S(1)}, bf16[256,1024]{1,0:T(8,128)(2,1)}, u32[]{:S(2)}) copy-start(bf16[256,1024]{1,0:T(8,128)(2,1)} %q_ref.1) | copy-start | bytes 1572868
  2.4 1.0 %copy-start.1 = (bf16[2,256,512]{2,1,0:T(8,128)(2,1)S(1)}, bf16[2,256,512]{2,1,0:T(8,128)(2,1)}, u32[]{:S(2)}) copy-start(bf16[2,256,512]{2,1,0:T(8,128)(2,1)} %kv_ref.1) | copy-start | bytes 1572868
  3.4 1.0 %copy-start.2 = (bf16[256,1024]{1,0:T(8,128)(2,1)S(1)}, bf16[256,1024]{1,0:T(8,128)(2,1)}, u32[]{:S(2)}) copy-start(bf16[256,1024]{1,0:T(8,128)(2,1)} %do_ref.1) | copy-start | bytes 1572868

commit v2 on v1

--- a/solution.py
+++ b/solution.py
@@ -30,12 +30,22 @@
 
 def kernel(
     n, rows, heads, group,
+    q_hbm, kv_hbm, do_hbm, doc_hbm,
+    att_ref, dq_ref, dkv_ref,
     q_ref, kv_ref, do_ref, doc_ref,
-    att_ref, dq_ref, dkv_ref,
     kv_in, doc_in, grad_out, grad_in, mask, exps, weights, own,
-    kv_send, kv_recv, doc_send, doc_recv, grad_send, grad_recv,
+    load_sem, kv_send, kv_recv, doc_send, doc_recv, grad_send, grad_recv,
 ):
     me = lax.axis_index("ctx")
+    loads = [
+        pltpu.make_async_copy(src, dst, load_sem.at[k])
+        for k, (src, dst) in enumerate(
+            ((kv_hbm, kv_ref), (doc_hbm, doc_ref), (q_hbm, q_ref), (do_hbm, do_ref))
+        )
+    ]
+    for load in loads:
+        load.start()
+
     barrier = pltpu.get_barrier_semaphore()
     for d in range(1, DEPTH + 1):
         @pl.when(me >= d)
@@ -51,7 +61,7 @@
 
     def doc_copy(d):
         return pltpu.make_async_remote_copy(
-            src_ref=doc_ref, dst_ref=doc_in.at[d - 1],
+            src_ref=doc_hbm, dst_ref=doc_in.at[d - 1],
             send_sem=doc_send.at[d - 1], recv_sem=doc_recv.at[d - 1],
             device_id={"ctx": me + d}, device_id_type=MESH,
         )
@@ -61,7 +71,7 @@
 
     def kv_copy(d, h):
         return pltpu.make_async_remote_copy(
-            src_ref=kv_ref.at[:, :, head_cols(h)], dst_ref=kv_in.at[d - 1, h],
+            src_ref=kv_hbm.at[:, :, head_cols(h)], dst_ref=kv_in.at[d - 1, h],
             send_sem=kv_send.at[d - 1, h], recv_sem=kv_recv.at[d - 1, h],
             device_id={"ctx": me + d}, device_id_type=MESH,
         )
@@ -93,6 +103,9 @@
         @pl.when(me + d >= n)
         def _(d=d):
             grad_in[d - 1] = jnp.zeros(grad_in.shape[1:], BF16)
+
+    for load in loads:
+        load.wait()
 
     query_doc = jnp.broadcast_to(doc_ref[...].astype(F32), (rows, rows))
 
@@ -225,9 +238,13 @@
             jax.ShapeDtypeStruct(queries.shape, BF16),
             jax.ShapeDtypeStruct(keys_values.shape, BF16),
         ),
-        in_specs=[vmem] * 4,
+        in_specs=[pl.BlockSpec(memory_space=pltpu.HBM)] * 4,
         out_specs=(vmem,) * 3,
         scratch_shapes=[
+            pltpu.VMEM(queries.shape, BF16),
+            pltpu.VMEM(keys_values.shape, BF16),
+            pltpu.VMEM(queries.shape, BF16),
+            pltpu.VMEM((1, rows), jnp.int32),
             pltpu.VMEM(slot, BF16),
             pltpu.VMEM((DEPTH, 1, rows), jnp.int32),
             pltpu.VMEM(slot, BF16),
@@ -236,12 +253,13 @@
             pltpu.VMEM((DEPTH + 1, rows, group * rows), BF16),
             pltpu.VMEM((DEPTH + 1, rows, group * rows), F32),
             pltpu.VMEM((heads, 2, rows, HD), F32),
+            dma((4,)),
             dma((DEPTH, heads)), dma((DEPTH, heads)),
             dma((DEPTH,)), dma((DEPTH,)),
             dma((DEPTH, heads)), dma((DEPTH, heads)),
         ],
         compiler_params=pltpu.CompilerParams(
-            collective_id=0, has_side_effects=True, vmem_limit_bytes=40 * 1024 * 1024
+            collective_id=0, has_side_effects=True, vmem_limit_bytes=63 * 1024 * 1024
         ),
         name="packed_attention",
     )(queries, keys_values, out_grad, doc_ids.reshape(1, rows))

time: 39.1 us -> 38.3 us (0.980)
  local copies, waits for them, and re-layouts: 6.18 us -> 3.95 us
  Pallas kernels: 32 us -> 33.5 us
    unnamed x11 -> x7, local copies, waits for them, and re-layouts: 6.18 us -> 3.95 us
    pallas_call x1, Pallas kernels: 32 us -> 33.5 us  [per_device(): pl.pallas_call(functools.partial(kernel, n, rows, heads, group), out_shap...]
where the time goes in v2:
time: 38.3 us; the launch traced here: 38.1 us
  Pallas kernels  33.5 us (87%)
  local copies, waits for them, and re-layouts  3.95 us (10%)
  between operations  0.65 us (2%)
    pallas_call x1, Pallas kernels, per_device(): pl.pallas_call(functools.partial(kernel, n, rows, heads, group), out_shap...  33.5 us
    unnamed x7, local copies, waits for them, and re-layouts  3.95 us

profile of v2, /device:TPU:0, one launch (start us, length us, event | category | flops | bytes accessed | tf_op | source)
XLA Modules:
  0.0 38.1 jit_solution(4724837386028402065)
XLA Ops:
  0.6 33.5 %packed_attention.1 = (bf16[256,1024]{1,0:T(8,128)(2,1)}, bf16[256,1024]{1,0:T(8,128)(2,1)}, bf16[2,256,512]{2,1,0:T(8,128)(2,1)}) custom-call(bf16[256,1024]{1,0:T(8,128)(2,1)} %q_hbm.1, bf16[2,256,512]{2,1,0:T(8,128)(2,1)} %kv_hbm.1, bf16[256,1024]{1,0:T(8,128)(2,1)} %do_hbm.1, s32[1,256]{1,0:T(1,128)} %bitcast.1), custom_call_target="tpu_custom_call" | custom-call | tf_op jit(solution)/shard_map/packed_attention/pallas_call | solution.py:234
  34.2 0.0 copy-start.1
  34.2 1.9 %copy.10 = bf16[256,1024]{1,0:T(8,128)(2,1)} copy(bf16[256,1024]{1,0:T(8,128)(2,1)} %get-tuple-element.6) | data formatting | bytes 1048576
  36.1 0.0 copy-done.1
  36.1 0.0 copy-start
  36.1 0.8 %copy.11 = bf16[256,1024]{1,0:T(8,128)(2,1)} copy(bf16[256,1024]{1,0:T(8,128)(2,1)S(1)} %copy-done.1) | data formatting | bytes 1048576
  36.9 0.4 %copy-done = bf16[2,256,512]{2,1,0:T(8,128)(2,1)S(1)} copy-done((bf16[2,256,512]{2,1,0:T(8,128)(2,1)S(1)}, bf16[2,256,512]{2,1,0:T(8,128)(2,1)}, u32[]{:S(2)}) %copy-start) | copy-done | bytes 524312
  37.3 0.8 %copy.12 = bf16[2,256,512]{2,1,0:T(8,128)(2,1)} copy(bf16[2,256,512]{2,1,0:T(8,128)(2,1)S(1)} %copy-done) | data formatting | bytes 1048576
Async XLA Ops:
  34.2 1.9 %copy-start.1 = (bf16[256,1024]{1,0:T(8,128)(2,1)S(1)}, bf16[256,1024]{1,0:T(8,128)(2,1)}, u32[]{:S(2)}) copy-start(bf16[256,1024]{1,0:T(8,128)(2,1)} %get-tuple-element.7) | copy-start | bytes 1572868
  36.1 1.2 %copy-start = (bf16[2,256,512]{2,1,0:T(8,128)(2,1)S(1)}, bf16[2,256,512]{2,1,0:T(8,128)(2,1)}, u32[]{:S(2)}) copy-start(bf16[2,256,512]{2,1,0:T(8,128)(2,1)} %get-tuple-element.8) | copy-start | bytes 1572868

commit v3 on v2

--- a/solution.py
+++ b/solution.py
@@ -76,10 +76,10 @@
             device_id={"ctx": me + d}, device_id_type=MESH,
         )
 
-    def grad_copy(d, h):
+    def grad_copy(d, h, which):
         return pltpu.make_async_remote_copy(
-            src_ref=grad_out.at[d - 1, h], dst_ref=grad_in.at[d - 1, h],
-            send_sem=grad_send.at[d - 1, h], recv_sem=grad_recv.at[d - 1, h],
+            src_ref=grad_out.at[d - 1, h, which], dst_ref=grad_in.at[d - 1, h, which],
+            send_sem=grad_send.at[d - 1, h, which], recv_sem=grad_recv.at[d - 1, h, which],
             device_id={"ctx": me - d}, device_id_type=MESH,
         )
 
@@ -165,22 +165,27 @@
         inverse_column = jnp.transpose(jnp.broadcast_to(inverse, (HD, width)))
         grads_scaled = (grads.astype(F32) * inverse_column).astype(BF16)
 
+        for d in range(DEPTH, 0, -1):
+            grad_out[d - 1, h, 1] = dot_nn(exps[d], grads_scaled).astype(BF16)
+
+            @pl.when(me >= d)
+            def _(d=d):
+                grad_copy(d, h, 1).start()
+
+        own[h, 1] = dot_nn(exps[0], grads_scaled)
         query_sum = jnp.zeros((HD, width), F32)
         for d in range(DEPTH, -1, -1):
             grad_prob = dot_nt(block(d, 1), grads)
             grad_logit = (weights[d] * ((grad_prob - grad_dot) * inverse)).astype(BF16)
             key_grad = dot_nn(grad_logit, queries) * SCORE_SCALE
-            value_grad = dot_nn(exps[d], grads_scaled)
             if d == 0:
                 own[h, 0] = key_grad
-                own[h, 1] = value_grad
             else:
                 grad_out[d - 1, h, 0] = key_grad.astype(BF16)
-                grad_out[d - 1, h, 1] = value_grad.astype(BF16)
 
                 @pl.when(me >= d)
                 def _(d=d):
-                    grad_copy(d, h).start()
+                    grad_copy(d, h, 0).start()
 
             query_sum = query_sum + dot_nn(jnp.transpose(block(d, 0)), grad_logit)
         query_grad = (query_sum * SCORE_SCALE).astype(BF16)
@@ -194,7 +199,8 @@
         for d in range(1, DEPTH + 1):
             @pl.when(me + d < n)
             def _(d=d):
-                grad_copy(d, h).wait_recv()
+                for which in range(2):
+                    grad_copy(d, h, which).wait_recv()
 
         total = own[h]
         for d in range(1, DEPTH + 1):
@@ -217,7 +223,8 @@
 
             @pl.when(me >= d)
             def _(d=d):
-                grad_copy(d, h).wait_send()
+                for which in range(2):
+                    grad_copy(d, h, which).wait_send()
         return carry
 
     lax.fori_loop(0, heads, drain, 0)
@@ -256,7 +263,7 @@
             dma((4,)),
             dma((DEPTH, heads)), dma((DEPTH, heads)),
             dma((DEPTH,)), dma((DEPTH,)),
-            dma((DEPTH, heads)), dma((DEPTH, heads)),
+            dma((DEPTH, heads, 2)), dma((DEPTH, heads, 2)),
         ],
         compiler_params=pltpu.CompilerParams(
             collective_id=0, has_side_effects=True, vmem_limit_bytes=63 * 1024 * 1024

time: 38.3 us -> 39 us (1.018)
  Pallas kernels: 33.5 us -> 34.2 us
    pallas_call x1, Pallas kernels: 33.5 us -> 34.2 us  [per_device(): pl.pallas_call(functools.partial(kernel, n, rows, heads, group), out_shap...]
where the time goes in v3:
time: 39 us; the launch traced here: 38.8 us
  Pallas kernels  34.2 us (88%)
  local copies, waits for them, and re-layouts  3.95 us (10%)
  between operations  0.65 us (2%)
    pallas_call x1, Pallas kernels, per_device(): pl.pallas_call(functools.partial(kernel, n, rows, heads, group), out_shap...  34.2 us
    unnamed x7, local copies, waits for them, and re-layouts  3.95 us

profile of v3, /device:TPU:0, one launch (start us, length us, event | category | flops | bytes accessed | tf_op | source)
XLA Modules:
  0.0 38.8 jit_solution(2769461342397902771)
XLA Ops:
  0.6 34.2 %packed_attention.1 = (bf16[256,1024]{1,0:T(8,128)(2,1)}, bf16[256,1024]{1,0:T(8,128)(2,1)}, bf16[2,256,512]{2,1,0:T(8,128)(2,1)}) custom-call(bf16[256,1024]{1,0:T(8,128)(2,1)} %q_hbm.1, bf16[2,256,512]{2,1,0:T(8,128)(2,1)} %kv_hbm.1, bf16[256,1024]{1,0:T(8,128)(2,1)} %do_hbm.1, s32[1,256]{1,0:T(1,128)} %bitcast.1), custom_call_target="tpu_custom_call" | custom-call | tf_op jit(solution)/shard_map/packed_attention/pallas_call | solution.py:241
  34.8 0.0 copy-start.1
  34.8 1.9 %copy.10 = bf16[256,1024]{1,0:T(8,128)(2,1)} copy(bf16[256,1024]{1,0:T(8,128)(2,1)} %get-tuple-element.6) | data formatting | bytes 1048576
  36.8 0.0 copy-done.1
  36.8 0.0 copy-start
  36.8 0.8 %copy.11 = bf16[256,1024]{1,0:T(8,128)(2,1)} copy(bf16[256,1024]{1,0:T(8,128)(2,1)S(1)} %copy-done.1) | data formatting | bytes 1048576
  37.6 0.4 %copy-done = bf16[2,256,512]{2,1,0:T(8,128)(2,1)S(1)} copy-done((bf16[2,256,512]{2,1,0:T(8,128)(2,1)S(1)}, bf16[2,256,512]{2,1,0:T(8,128)(2,1)}, u32[]{:S(2)}) %copy-start) | copy-done | bytes 524312
  38.0 0.8 %copy.12 = bf16[2,256,512]{2,1,0:T(8,128)(2,1)} copy(bf16[2,256,512]{2,1,0:T(8,128)(2,1)S(1)} %copy-done) | data formatting | bytes 1048576
Async XLA Ops:
  34.8 1.9 %copy-start.1 = (bf16[256,1024]{1,0:T(8,128)(2,1)S(1)}, bf16[256,1024]{1,0:T(8,128)(2,1)}, u32[]{:S(2)}) copy-start(bf16[256,1024]{1,0:T(8,128)(2,1)} %get-tuple-element.7) | copy-start | bytes 1572868
  36.8 1.2 %copy-start = (bf16[2,256,512]{2,1,0:T(8,128)(2,1)S(1)}, bf16[2,256,512]{2,1,0:T(8,128)(2,1)}, u32[]{:S(2)}) copy-start(bf16[2,256,512]{2,1,0:T(8,128)(2,1)} %get-tuple-element.8) | copy-start | bytes 1572868
